TPU v7x, 32 devices: a whole 2x2x4 slice. The times are simulated.
32 devices in a mesh: grp: 2 (over y), row: 4 (over z), col: 4 (over x, core).
Axes of the slice: x: 2, y: 2, z: 4, core: 2. Of those that a mesh axis runs over, the one named last changes fastest.
Arguments:
- pair_map: bfloat16 [256, 128, 128], P(('grp', 'row'), 'col'), parts along dimension 0, may hold values from -6 to 6
- pair_mask: int32 [256, 128], P(('grp', 'row'), 'col'), parts along dimension 0, may hold values from 0 to 1, as said below
- input_gain: float32 [128], replicated, may hold values from 0.1 to 1.9
- input_weight: bfloat16 [128, 640], replicated, may hold values from -0.5 to 0.5
- middle_gain: float32 [128], replicated, may hold values from 0.1 to 1.9
- output_weight: bfloat16 [128, 128], replicated, may hold values from -0.5 to 0.5
Outputs:
- update: bfloat16 [256, 128, 128], P(('grp', 'row'), 'col'), parts along dimension 0
There are 2 independent parts, one for each index of `grp`. A program takes and returns all parts, laid end to end along the dimension named above; an argument that names none is the same for every part. Nothing has to cross between parts.
Inputs may be any that keep to these rules, and one draw needn't show every extreme that they name: pair_mask[i, j] is 1 exactly where both i and j lie before the complex's padding tail, which begins at a residue of at least 64.
All inputs are finite; a program needn't handle non-finite values.
Results may differ from a plain program's by a relative error of at most 0.0078.
Values may be sent and summed in bfloat16 or wider, within the bound.
A program may use at most 64 MiB of HBM per device.

v0:
```python
import jax
import jax.numpy as jnp
from jax import lax
from jax.sharding import PartitionSpec as P

epsilon = 1e-05


def spread_2(x, axis, root):
    mine = lax.axis_index(axis) == root
    return lax.psum(jnp.where(mine, x, jnp.zeros_like(x)), axis)


def normalize(values, gain_vector):
    center = values - jnp.mean(values, axis=-1, keepdims=True)
    spread = jnp.mean(center * center, axis=-1, keepdims=True)
    return center * lax.rsqrt(spread + epsilon) * gain_vector


def gated_product(normed, weight_pair, mask_column):
    both_halves = jnp.dot(normed, weight_pair, preferred_element_type=jnp.float32)
    half_width = both_halves.shape[1] // 2
    return (
        mask_column * jax.nn.sigmoid(both_halves[:, :half_width]) * both_halves[:, half_width:]
    ).astype(jnp.bfloat16)


def body(pair_map, pair_mask, input_gain, input_weight, middle_gain, output_weight):
    row_count, column_count, channels = pair_map.shape
    hidden = output_weight.shape[0]
    flat_pairs = pair_map.reshape(row_count * column_count, channels).astype(jnp.float32)
    normed = normalize(flat_pairs, input_gain).astype(jnp.bfloat16)
    mask_column = pair_mask.reshape(-1, 1).astype(jnp.float32)
    left_block = gated_product(normed, input_weight[:, : 2 * hidden], mask_column).reshape(
        row_count, column_count, hidden
    )
    right_block = gated_product(
        normed, input_weight[:, 2 * hidden : 4 * hidden], mask_column
    ).reshape(row_count, column_count, hidden)
    column_devices = lax.axis_size("col")
    row_devices = lax.axis_size("row")
    owners = column_devices // 4
    spread_factor = column_devices // row_devices
    column_index = lax.axis_index("col")
    owner_row = column_index // spread_factor
    offset = column_index % spread_factor * column_count

    def panel_step(sender, running):
        left_piece, right_piece = (
            spread_2(left_block, "col", sender),
            spread_2(right_block, "col", sender),
        )
        mirror_piece = lax.dynamic_slice_in_dim(right_piece, offset, column_count, 0)
        mirror_piece = spread_2(mirror_piece, "row", owner_row)
        return running + jnp.einsum(
            "ikh,jkh->ijh", left_piece, mirror_piece, preferred_element_type=jnp.float32
        )

    initial = jnp.zeros((row_count, column_count, hidden), jnp.float32)
    product = lax.fori_loop(0, owners, panel_step, initial)
    middle = normalize(product.reshape(-1, hidden), middle_gain).astype(jnp.bfloat16)
    gate_values = jax.nn.sigmoid(
        jnp.dot(normed, input_weight[:, 4 * hidden :], preferred_element_type=jnp.float32)
    )
    update = gate_values * jnp.dot(middle, output_weight, preferred_element_type=jnp.float32)
    return update.astype(jnp.bfloat16).reshape(row_count, column_count, channels)


def solution(mesh):
    placed = (P(("grp", "row"), "col", None), P(("grp", "row"), "col"), P(), P(), P(), P())
    return jax.shard_map(
        body, mesh=mesh, in_specs=placed, out_specs=P(("grp", "row"), "col", None), check_vma=False
    )
```

profile of v0, /device:TPU:3, one launch (start us, length us, event | category | flops | bytes accessed | tf_op | source)
XLA Modules:
  0.0 137.0 jit_solution(282701240482753748)
XLA Ops:
  6.5 0.0 copy-start
  6.5 0.0 copy-start.3
  6.5 0.0 copy-start.4
  6.5 0.0 all-reduce.6.cloned.1.call-start
  6.5 1.2 convert_reduce_fusion
  7.8 1.3 multiply_reduce_fusion.1
  9.1 0.1 div.28
  9.2 0.1 rsqrt.23
  9.2 1.3 fusion.19
  10.5 1.1 fusion.20
  11.7 0.0 copy-done.3
  11.7 0.3 fusion.22
  12.0 0.0 copy-done.4
  12.0 0.1 convert_element_type.41
  12.0 0.4 broadcast_select_fusion.1
  12.4 2.3 %copy.22 = bf16[32,32,128]{1,0,2:T(8,128)(2,1)} copy(bf16[32,32,128]{2,1,0:T(8,128)(2,1)S(1)} %bitcast.29) | data formatting | bytes 524288 | tf_op jit(solution)/shard_map/while/body/eval_jaxpr/jit(_where)/select_n | solution.py:11
  14.7 2.3 %copy.23 = bf16[32,32,128]{1,0,2:T(8,128)(2,1)} copy(bf16[32,32,128]{2,1,0:T(8,128)(2,1)S(1)} %bitcast.28) | data formatting | bytes 524288 | tf_op jit(solution)/shard_map/while/body/eval_jaxpr/jit(_where)/select_n | solution.py:11
  17.1 0.0 all-reduce.6.cloned.1.call-update
  17.1 0.0 all-reduce.4.cloned.1.call-start
  17.1 52.0 %all-reduce.6.cloned.1.call-done = (bf16[32,32,128]{1,0,2:T(8,128)(2,1)}, bf16[32,32,128]{1,0,2:T(8,128)(2,1)}) async-done(((bf16[32,32,128]{1,0,2:T(8,128)(2,1)}, bf16[32,32,128]{1,0,2:T(8,128)(2,1)}), (bf16[32,32,128]{1,0,2:T(8,128)(2,1)}, bf16[32,32,128]{1,0,2:T(8,128)(2,1)})) %all-reduce.6.cloned.1.call-update) | async-done | bytes 524304 | tf_op jit(solution)/shard_map/while/body/eval_jaxpr/psum | solution.py:11
  69.2 1.1 broadcast_select_fusion
  70.2 0.0 copy-start.1
  70.2 0.0 all-reduce.4.cloned.1.call-update
  70.3 1.1 fusion.2
  71.3 53.3 %all-reduce.4.cloned.1.call-done = bf16[32,32,128]{1,0,2:T(8,128)(2,1)} async-done(((bf16[32,32,128]{1,0,2:T(8,128)(2,1)}), bf16[32,32,128]{1,0,2:T(8,128)(2,1)}) %all-reduce.4.cloned.1.call-update) | async-done | bytes 262160 | tf_op jit(solution)/shard_map/while/body/eval_jaxpr/psum | solution.py:11
  124.7 0.0 copy-done.1
  124.7 1.9 %fusion.25 = (f32[32,32]{0,1:T(8,128)S(1)}, f32[32,32,128]{0,1,2:T(8,128)S(1)}) fusion(bf16[32,32,128]{1,0,2:T(8,128)(2,1)} %all-reduce.4.cloned.1.call-done, bf16[32,32,128]{1,0,2:T(8,128)(2,1)S(1)} %copy-done.1), kind=kOutput, calls=%fused_computation.44 | convolution fusion | flops 8518656 | bytes 1052672 | tf_op jit(solution)/shard_map/while/body/eval_jaxpr/ikh,jkh->ijh/dot_general | solution.py:55
  126.6 0.1 copy.25
  126.6 0.1 copy.26
  126.7 0.1 div.34
  126.8 0.0 copy-start.5
  126.8 1.4 %copy.24 = f32[32,32,128]{2,1,0:T(8,128)S(1)} copy(f32[32,32,128]{0,1,2:T(8,128)S(1)} %get-tuple-element.30) | data formatting | bytes 1048576 | tf_op jit(solution)/shard_map/while/body/eval_jaxpr/ikh,jkh->ijh/transpose | solution.py:55
  128.2 0.0 copy-start.2
  128.2 0.3 multiply_reduce_fusion
  128.6 0.1 copy.27
  128.7 0.1 rsqrt.25
  128.7 0.0 copy-done.5
  128.7 0.3 fusion.16
  129.1 0.0 copy-done
  129.1 0.2 copy-done.2
  129.3 0.9 fusion.3
  (5 shorter events, 0.0 us)
Async XLA Ops:
  6.5 122.5 %copy-start = (bf16[128,128]{1,0:T(8,128)(2,1)S(1)}, bf16[128,128]{1,0:T(8,128)(2,1)}, u32[]{:S(2)}) copy-start(bf16[128,128]{1,0:T(8,128)(2,1)} %param.11) | copy-start | bytes 98308
  6.5 5.1 %copy-start.3 = (bf16[128,640]{1,0:T(8,128)(2,1)S(1)}, bf16[128,640]{1,0:T(8,128)(2,1)}, u32[]{:S(2)}) copy-start(bf16[128,640]{1,0:T(8,128)(2,1)} %param.9) | copy-start | bytes 491524
  6.5 5.4 %copy-start.4 = (s32[32,32]{1,0:T(8,128)S(1)}, s32[32,32]{1,0:T(8,128)}, u32[]{:S(2)}) copy-start(s32[32,32]{1,0:T(8,128)} %param.7) | copy-start | bytes 12292
  6.5 62.6 %all-reduce.6.cloned.1.call-start = ((), (), s32[]{:S(2)}) async-start(), calls=%async_computation.1 | async-start | bytes 4194304 | tf_op jit(solution)/shard_map/while/body/eval_jaxpr/psum | solution.py:11
  17.1 107.6 %all-reduce.4.cloned.1.call-start = ((), (), s32[]{:S(2)}) async-start(), calls=%async_computation | async-start | bytes 2097152 | tf_op jit(solution)/shard_map/while/body/eval_jaxpr/psum | solution.py:11
  70.2 54.4 %copy-start.1 = (bf16[32,32,128]{1,0,2:T(8,128)(2,1)S(1)}, bf16[32,32,128]{1,0,2:T(8,128)(2,1)}, u32[]{:S(2)}) copy-start(bf16[32,32,128]{1,0,2:T(8,128)(2,1)} %get-tuple-element.18) | copy-start | bytes 786436
  126.8 1.9 %copy-start.5 = (f32[128]{0:T(128)S(1)}, f32[128]{0:T(128)}, u32[]{:S(2)}) copy-start(f32[128]{0:T(128)} %param.10) | copy-start | bytes 1540
  128.2 1.1 copy-start.2
Sparse Core Ops, SparseCore 0:
  17.2 51.9 all-reduce.5
  71.7 52.9 all-reduce.3
where the time goes:
time: 139 us; the launch traced here: 137 us
  waiting for transfers between devices  105 us (76%)
  between operations  13.5 us (10%)
  local copies, waits for them, and re-layouts  6.83 us (5%)
  other arithmetic  5.96 us (4%)
  matrix products  5.27 us (4%)
    psum x2, waiting for transfers between devices, spread_2(): return lax.psum(jnp.where(mine, x, jnp.zeros_like(x)), axis)  105 us
    select_n x2, local copies, waits for them, and re-layouts, spread_2(): return lax.psum(jnp.where(mine, x, jnp.zeros_like(x)), axis)  4.62 us
  transfers between devices with their start and end apart: 2, of which 2 were waited for; matrix products, arithmetic and copies ran while one was open for 1% of the time, Pallas kernels for 0%

commit v1 on v0

v1 whole, which is shorter than its diff:
```python
import functools

import jax
import jax.numpy as jnp
from jax import lax
from jax.experimental import pallas as pl
from jax.experimental.pallas import tpu as pltpu
from jax.sharding import PartitionSpec as P

epsilon = 1e-05
MESH = pl.DeviceIdType.MESH


def normalize(values, gain_vector):
    center = values - jnp.mean(values, axis=-1, keepdims=True)
    spread = jnp.mean(center * center, axis=-1, keepdims=True)
    return center * lax.rsqrt(spread + epsilon) * gain_vector


def sigmoid(values):
    return 0.5 * jnp.tanh(0.5 * values) + 0.5


def gated_product(rows, gain, weight_pair):
    normed = normalize(rows.astype(jnp.float32), gain).astype(jnp.bfloat16)
    both = jnp.dot(normed, weight_pair, preferred_element_type=jnp.float32)
    half = both.shape[1] // 2
    return sigmoid(both[:, :half]) * both[:, half:]


def kernel(
    sizes, x_hbm, mask_ref, gain_ref, w_ref, mgain_ref, wout_ref, out_ref,
    own, abuf, bbuf, left, right, swapped, gate, product,
    own_sem, keep_sem, asend, arecv, fwd_send, bsend, brecv, take_sem,
):
    rows, cols, owners, n_row, n_col, hid = sizes
    spread = n_col // n_row
    depth = owners * cols
    half = rows // 2
    part = cols // 2
    r, c = lax.axis_index("row"), lax.axis_index("col")
    root = c // spread
    is_root = r == root
    offset = (c % spread) * cols
    chip = c // 2
    sibling = c + 1 - 2 * (c % 2)
    is_owner = c < owners
    owner_chips = (owners + 1) // 2

    own_copy = pltpu.make_async_copy(x_hbm, own, own_sem)
    own_copy.start()

    barrier = pltpu.get_barrier_semaphore()
    forwards = (chip != 0) if owner_chips == 1 else (chip >= 0)
    for o in range(owners):
        @pl.when(c != o)
        def _():
            pl.semaphore_signal(barrier, inc=1, device_id={"col": o}, device_id_type=MESH)

    @pl.when(forwards)
    def _():
        pl.semaphore_signal(barrier, inc=1, device_id={"col": sibling}, device_id_type=MESH)

    above = r > root
    upstream = jnp.where(above, r - 1, r + 1)
    upstream = jnp.clip(upstream, 0, n_row - 1)

    @pl.when(jnp.logical_not(is_root))
    def _():
        pl.semaphore_signal(barrier, inc=1, device_id={"row": upstream}, device_id_type=MESH)

    goes_up = jnp.logical_and(r >= root, r + 1 < n_row)
    goes_down = jnp.logical_and(r <= root, r >= 1)
    awaited = (
        jnp.where(is_owner, n_col - 1, 0)
        + forwards.astype(jnp.int32)
        + goes_up.astype(jnp.int32)
        + goes_down.astype(jnp.int32)
    )

    @pl.when(awaited > 0)
    def _():
        pl.semaphore_wait(barrier, awaited)

    def a_copy(o, h, target):
        return pltpu.make_async_remote_copy(
            src_ref=x_hbm.at[pl.ds(h * half, half)],
            dst_ref=abuf.at[o, pl.ds(h * half, half)],
            send_sem=asend.at[target, h],
            recv_sem=arecv.at[o, h],
            device_id={"col": target},
            device_id_type=MESH,
        )

    def sibling_copy(o, h):
        return pltpu.make_async_remote_copy(
            src_ref=abuf.at[o, pl.ds(h * half, half)],
            dst_ref=abuf.at[o, pl.ds(h * half, half)],
            send_sem=fwd_send.at[o, h],
            recv_sem=arecv.at[o, h],
            device_id={"col": sibling},
            device_id_type=MESH,
        )

    def b_copy(o, q, way, from_root):
        target = jnp.clip(r + way, 0, n_row - 1)
        if from_root:
            source = abuf.at[o, pl.ds(offset + q * part, part)]
        else:
            source = bbuf.at[o, pl.ds(q * part, part)]
        return pltpu.make_async_remote_copy(
            src_ref=source,
            dst_ref=bbuf.at[o, pl.ds(q * part, part)],
            send_sem=bsend.at[o, q, (way + 1) // 2],
            recv_sem=brecv.at[o, q],
            device_id={"row": target},
            device_id_type=MESH,
        )

    keep = [pltpu.make_async_copy(x_hbm, abuf.at[o], keep_sem.at[o]) for o in range(owners)]
    for o in range(owners):
        @pl.when(c == o)
        def _():
            keep[o].start()
            for h in range(2):
                for target in range(n_col):
                    if target == o or (target // 2 != o // 2 and target % 2 != h):
                        continue
                    a_copy(o, h, target).start()

    own_copy.wait()
    step = 8

    def gate_step(t, carry):
        at = pl.ds(t * step, step)
        mask = mask_ref[at, :].astype(jnp.float32)
        flat = own[at].reshape(step * cols, -1)
        normed = normalize(flat.astype(jnp.float32), gain_ref[...]).astype(jnp.bfloat16)
        values = sigmoid(
            jnp.dot(normed, w_ref[:, 4 * hid :], preferred_element_type=jnp.float32)
        )
        values = values.reshape(step, cols, -1) * mask[:, :, None]
        gate[at] = values
        return carry

    lax.fori_loop(0, rows // step, gate_step, 0)

    def left_rows(o, first, count):
        def go(t, carry):
            at = first + t * step
            values = gated_product(
                abuf[o, pl.ds(at, step)].reshape(step * cols, -1), gain_ref[...], w_ref[:, : 2 * hid]
            )
            left[pl.ds(at, step), o] = values.reshape(step, cols, hid)
            return carry
        lax.fori_loop(0, count // step, go, 0)

    def start_b(o, q):
        @pl.when(jnp.logical_and(is_root, goes_up))
        def _():
            b_copy(o, q, 1, True).start()

        @pl.when(jnp.logical_and(is_root, goes_down))
        def _():
            b_copy(o, q, -1, True).start()

    for o in range(owners):
        @pl.when(c == o)
        def _():
            keep[o].wait()
        for h in range(2):
            @pl.when(c != o)
            def _():
                a_copy(o, h, 0).wait_recv()

            @pl.when(jnp.logical_and(chip != o // 2, c % 2 == h))
            def _():
                sibling_copy(o, h).start()

            if spread == 1:
                start_b(o, h)
        if spread != 1:
            for q in range(2):
                start_b(o, q)

    for o in range(owners):
        left_rows(o, 0, rows)

    def right_rows(o, q):
        def go(t, carry):
            at = q * part + t * step
            values = gated_product(
                bbuf[o, pl.ds(at, step)].reshape(step * cols, -1),
                gain_ref[...],
                w_ref[:, 2 * hid : 4 * hid],
            )
            right[pl.ds(t * step * cols, step * cols)] = values
            return carry
        lax.fori_loop(0, part // step, go, 0)

        def swap(k, carry):
            swapped[o * cols + k] = right[pl.ds(k, part, stride=cols), :]
            return carry
        lax.fori_loop(0, cols, swap, 0, unroll=8)

    for q in range(2):
        for o in range(owners):
            @pl.when(jnp.logical_not(is_root))
            def _():
                b_copy(o, q, 1, False).wait_recv()

                @pl.when(goes_up)
                def _():
                    b_copy(o, q, 1, False).start()

                @pl.when(goes_down)
                def _():
                    b_copy(o, q, -1, False).start()

            @pl.when(is_root)
            def _():
                take = pltpu.make_async_copy(
                    abuf.at[o, pl.ds(offset + q * part, part)],
                    bbuf.at[o, pl.ds(q * part, part)],
                    take_sem.at[o, q],
                )
                take.start()
                take.wait()
            right_rows(o, q)

        band = 8

        def multiply(t, carry):
            for j in range(0, part, 16):
                sums = [jnp.zeros((16, hid), jnp.float32) for _ in range(band)]

                def add(k8, sums):
                    sums = list(sums)
                    o = k8 // (cols // 8)
                    kk = (k8 % (cols // 8)) * 8
                    for k in range(8):
                        other = swapped[k8 * 8 + k, j : j + 16]
                        for i in range(band):
                            mine = left[t * band + i, o, pl.ds(kk + k, 1), :]
                            sums[i] = sums[i] + mine * other
                    return tuple(sums)

                sums = lax.fori_loop(0, depth // 8, add, tuple(sums))
                for i in range(band):
                    product[i, j : j + 16] = sums[i]
            at = pl.ds(t * band, band)
            flat = product[...].reshape(band * part, hid)
            middle = normalize(flat, mgain_ref[...]).astype(jnp.bfloat16)
            update = jnp.dot(middle, wout_ref[...], preferred_element_type=jnp.float32)
            update = update.reshape(band, part, -1) * gate[at, q * part : (q + 1) * part]
            out_ref[at, q * part : (q + 1) * part] = update.astype(jnp.bfloat16)
            return carry

        lax.fori_loop(0, rows // band, multiply, 0)

    for o in range(owners):
        @pl.when(c == o)
        def _():
            for h in range(2):
                for target in range(n_col):
                    if target == o or (target // 2 != o // 2 and target % 2 != h):
                        continue
                    a_copy(o, h, target).wait_send()
        for h in range(2):
            @pl.when(jnp.logical_and(chip != o // 2, c % 2 == h))
            def _():
                sibling_copy(o, h).wait_send()

            @pl.when(goes_up)
            def _():
                b_copy(o, h, 1, False).wait_send()

            @pl.when(goes_down)
            def _():
                b_copy(o, h, -1, False).wait_send()


def body(mesh_sizes, pair_map, pair_mask, input_gain, input_weight, middle_gain, output_weight):
    n_row, n_col = mesh_sizes
    rows, cols, channels = pair_map.shape
    hid = output_weight.shape[0]
    owners = n_col // 4
    part = cols // 2
    vmem = pl.BlockSpec(memory_space=pltpu.VMEM)
    sizes = (rows, cols, owners, n_row, n_col, hid)
    f32, bf16 = jnp.float32, jnp.bfloat16
    dma = pltpu.SemaphoreType.DMA
    return pl.pallas_call(
        functools.partial(kernel, sizes),
        out_shape=jax.ShapeDtypeStruct(pair_map.shape, bf16),
        in_specs=[pl.BlockSpec(memory_space=pl.ANY)] + [vmem] * 5,
        out_specs=vmem,
        scratch_shapes=[
            pltpu.VMEM((rows, cols, channels), bf16),
            pltpu.VMEM((owners, rows, cols, channels), bf16),
            pltpu.VMEM((owners, cols, cols, channels), bf16),
            pltpu.VMEM((rows, owners, cols, hid), f32),
            pltpu.VMEM((part * cols, hid), f32),
            pltpu.VMEM((owners * cols, part, hid), f32),
            pltpu.VMEM((rows, cols, channels), f32),
            pltpu.VMEM((8, part, hid), f32),
            dma,
            dma((owners,)),
            dma((n_col, 2)),
            dma((owners, 2)),
            dma((owners, 2)),
            dma((owners, 2, 2)),
            dma((owners, 2)),
            dma((owners, 2)),
        ],
        compiler_params=pltpu.CompilerParams(
            collective_id=0, has_side_effects=True, vmem_limit_bytes=56 * 2**20
        ),
    )(
        pair_map,
        pair_mask,
        input_gain.reshape(1, -1),
        input_weight,
        middle_gain.reshape(1, -1),
        output_weight,
    )


def solution(mesh):
    placed = (P(("grp", "row"), "col", None), P(("grp", "row"), "col"), P(), P(), P(), P())
    return jax.shard_map(
        functools.partial(body, (mesh.shape["row"], mesh.shape["col"])),
        mesh=mesh,
        in_specs=placed,
        out_specs=P(("grp", "row"), "col", None),
        check_vma=False,
    )
```

time: 139 us -> 27.8 us (0.20); the launches traced: 137 us -> 27.6 us
  waiting for transfers between devices: 105 us -> 0 us
  Pallas kernels: 0 us -> 26 us
  between operations: 13.5 us -> 0.01 us
  other arithmetic: 5.96 us -> 0 us
  matrix products: 5.27 us -> 0 us
  local copies, waits for them, and re-layouts: 6.83 us -> 1.67 us
    psum x2 -> x0, waiting for transfers between devices: 105 us -> none  [spread_2(): return lax.psum(jnp.where(mine, x, jnp.zeros_like(x)), axis)]
    pallas_call x0 -> x1, Pallas kernels: none -> 26 us  [body(): pl.pallas_call(functools.partial(kernel, sizes), out_shape=jax.ShapeDtype...]
    dot_general x5 -> x0, matrix products: 5.27 us -> none  [the longest x1 1.89 us: panel_step(): jnp.einsum('ikh,jkh->ijh', left_piece, mirror_piece, preferred_element_ty...]
    select_n x2 -> x0, local copies, waits for them, and re-layouts: 4.62 us -> none  [spread_2(): return lax.psum(jnp.where(mine, x, jnp.zeros_like(x)), axis)]
    reduce_sum x3 -> x0, other arithmetic: 2.85 us -> none  [the longest x2 1.66 us: normalize(): spread = jnp.mean(center * center, axis=-1, keepdims=True)]
    convert_element_type x3 -> x0, other arithmetic: 1.64 us -> none  [the longest x1 1.29 us: body(): normed = normalize(flat_pairs, input_gain).astype(jnp.bfloat16)]
    unnamed x12 -> x1, local copies, waits for them, and re-layouts: 0.21 us -> 1.67 us
    select_n x2 -> x0, other arithmetic: 1.44 us -> none  [spread_2(): return lax.psum(jnp.where(mine, x, jnp.zeros_like(x)), axis)]
  transfers between devices with their start and end apart: 2 -> 0, of which waited for: 2 -> 0; matrix products, arithmetic and copies ran while one was open for 1% -> 0% of each run, Pallas kernels for 0% -> 0%
where the time goes in v1:
time: 27.8 us; the launch traced here: 27.6 us
  Pallas kernels  26 us (94%)
  local copies, waits for them, and re-layouts  1.67 us (6%)
    pallas_call x1, Pallas kernels, body(): pl.pallas_call(functools.partial(kernel, sizes), out_shape=jax.ShapeDtype...  26 us
    unnamed x1, local copies, waits for them, and re-layouts  1.67 us

profile of v1, /device:TPU:3, one launch (start us, length us, event | category | flops | bytes accessed | tf_op | source)
XLA Modules:
  0.0 27.6 jit_solution(11746520535927321444)
XLA Ops:
  0.0 26.0 %shard_map.64 = bf16[32,32,128]{2,1,0:T(8,128)(2,1)} custom-call(bf16[32,32,128]{2,1,0:T(8,128)(2,1)} %x_hbm.1, s32[32,32]{1,0:T(8,128)} %mask_ref.1, f32[1,128]{1,0:T(1,128)} %bitcast.2, bf16[128,640]{1,0:T(8,128)(2,1)} %w_ref.1, f32[1,128]{1,0:T(1,128)} %bitcast.3, bf16[128,128]{1,0:T(8,128)(2,1)} %wout_ref.1), custom_call_target="tpu_custom_call" | custom-call | tf_op jit(solution)/shard_map/pallas_call | solution.py:293
  26.0 1.7 %copy.8 = bf16[32,32,128]{2,1,0:T(8,128)(2,1)} copy(bf16[32,32,128]{2,1,0:T(8,128)(2,1)} %shard_map.64) | data formatting | bytes 524288

commit v2 on v1

v2 whole, which is shorter than its diff:
```python
import functools

import jax
import jax.numpy as jnp
from jax import lax
from jax.experimental import pallas as pl
from jax.experimental.pallas import tpu as pltpu
from jax.sharding import PartitionSpec as P

epsilon = 1e-05
MESH = pl.DeviceIdType.MESH
CHUNKS = 4


def normalize(values, gain_vector):
    center = values - jnp.mean(values, axis=-1, keepdims=True)
    spread = jnp.mean(center * center, axis=-1, keepdims=True)
    return center * lax.rsqrt(spread + epsilon) * gain_vector


def sigmoid(values):
    return 0.5 * jnp.tanh(0.5 * values) + 0.5


def gated_product(rows, gain, weight_pair):
    normed = normalize(rows.astype(jnp.float32), gain).astype(jnp.bfloat16)
    both = jnp.dot(normed, weight_pair, preferred_element_type=jnp.float32)
    half = both.shape[1] // 2
    return sigmoid(both[:, :half]) * both[:, half:]


def kernel(
    sizes, x_hbm, mask_ref, gain_ref, w_ref, mgain_ref, wout_ref, out_ref,
    own, abuf, bbuf, left, right, swapped, gate, product,
    own_sem, keep_sem, asend, arecv, fwd_send, bsend, brecv, take_sem,
):
    rows, cols, owners, n_row, n_col, hid = sizes
    spread = n_col // n_row
    depth = owners * cols
    tall = rows // CHUNKS
    part = cols // CHUNKS
    r, c = lax.axis_index("row"), lax.axis_index("col")
    root = c // spread
    is_root = r == root
    chip = c // 2
    sibling = c + 1 - 2 * (c % 2)
    partner = c + 2 - 4 * ((c // 2) % 2)
    partner_root = partner // spread
    middle_row = n_row // 2

    def crosses(one, other):
        return (one >= middle_row) != (other >= middle_row)

    own_copy = pltpu.make_async_copy(x_hbm, own, own_sem)
    own_copy.start()

    barrier = pltpu.get_barrier_semaphore()
    owner_chips = (owners + 1) // 2
    forwards = (chip != 0) if owner_chips == 1 else (chip >= 0)

    def greet(where):
        pl.semaphore_signal(barrier, inc=1, device_id=where, device_id_type=MESH)

    @pl.when(jnp.logical_not(is_root))
    def _():
        greet({"row": root})

    @pl.when(crosses(r, root))
    def _():
        greet({"row": root, "col": partner})

    for o in range(owners):
        @pl.when(c != o)
        def _():
            greet({"col": o})

    @pl.when(forwards)
    def _():
        greet({"col": sibling})

    helps = r == partner_root
    awaited = (
        jnp.where(c < owners, n_col - 1, 0)
        + forwards.astype(jnp.int32)
        + jnp.where(is_root, n_row - 1, 0)
        + jnp.where(helps, middle_row, 0)
    )

    @pl.when(awaited > 0)
    def _():
        pl.semaphore_wait(barrier, awaited)

    def a_copy(o, q, target):
        return pltpu.make_async_remote_copy(
            src_ref=x_hbm.at[pl.ds(q * tall, tall)],
            dst_ref=abuf.at[o, pl.ds(q * tall, tall)],
            send_sem=asend.at[target, q],
            recv_sem=arecv.at[o, q],
            device_id={"col": target},
            device_id_type=MESH,
        )

    def sibling_copy(o, q):
        return pltpu.make_async_remote_copy(
            src_ref=abuf.at[o, pl.ds(q * tall, tall)],
            dst_ref=abuf.at[o, pl.ds(q * tall, tall)],
            send_sem=fwd_send.at[o, q],
            recv_sem=arecv.at[o, q],
            device_id={"col": sibling},
            device_id_type=MESH,
        )

    def b_copy(o, q, row, helping, from_own=False):
        column = partner if helping else c
        at = pl.ds((column % spread) * cols + q * part, part)
        return pltpu.make_async_remote_copy(
            src_ref=x_hbm.at[at] if from_own else abuf.at[o, at],
            dst_ref=bbuf.at[o, pl.ds(q * part, part)],
            send_sem=bsend.at[o, q, int(helping), row],
            recv_sem=brecv.at[o, q],
            device_id={"row": row, "col": column},
            device_id_type=MESH,
        )

    def each_b(o, q, act):
        for row in range(n_row):
            direct = jnp.logical_and(is_root, root != row)
            if q % 2:
                direct = jnp.logical_and(direct, jnp.logical_not(crosses(root, row)))

                @pl.when(jnp.logical_and(helps, crosses(partner_root, row)))
                def _():
                    act(o, q, row, True)

            @pl.when(direct)
            def _():
                act(o, q, row, False)

    def start_b(o, q):
        @pl.when(c == o)
        def _():
            each_b(o, q, lambda *at: b_copy(*at, from_own=True).start())

        @pl.when(c != o)
        def _():
            each_b(o, q, lambda *at: b_copy(*at).start())

    keep = [pltpu.make_async_copy(x_hbm, abuf.at[o], keep_sem.at[o]) for o in range(owners)]

    def each_a(o, q, act):
        for target in range(n_col):
            if target == o or (target // 2 != o // 2 and target % 2 != q % 2):
                continue
            act(o, q, target)

    for o in range(owners):
        @pl.when(c == o)
        def _():
            keep[o].start()
            for q in range(CHUNKS):
                each_a(o, q, lambda *at: a_copy(*at).start())

    for o in range(owners):
        for q in range(CHUNKS):
            @pl.when(c != o)
            def _():
                a_copy(o, q, 0).wait_recv()

            @pl.when(jnp.logical_and(chip != o // 2, c % 2 == q % 2))
            def _():
                sibling_copy(o, q).start()

            if spread == 1:
                start_b(o, q)
        if spread != 1:
            for q in range(CHUNKS):
                start_b(o, q)

        @pl.when(c == o)
        def _():
            keep[o].wait()

        @pl.when(is_root)
        def _():
            take_copy(abuf, bbuf, take_sem, o, (c % spread) * cols, cols).start()

    own_copy.wait()
    step = min(rows, max(1, 512 // cols))

    def gate_step(t, carry):
        at = pl.ds(t * step, step)
        mask = mask_ref[at, :].astype(jnp.float32)
        flat = own[at].reshape(step * cols, -1)
        normed = normalize(flat.astype(jnp.float32), gain_ref[...]).astype(jnp.bfloat16)
        values = sigmoid(
            jnp.dot(normed, w_ref[:, 4 * hid :], preferred_element_type=jnp.float32)
        )
        gate[at] = values.reshape(step, cols, -1) * mask[:, :, None]
        return carry

    lax.fori_loop(0, rows // step, gate_step, 0)

    for o in range(owners):
        def left_step(t, carry):
            at = pl.ds(t * step, step)
            values = gated_product(
                abuf[o, at].reshape(step * cols, -1), gain_ref[...], w_ref[:, : 2 * hid]
            )
            left[at, o] = values.reshape(step, cols, hid)
            return carry

        lax.fori_loop(0, rows // step, left_step, 0)

    for o in range(owners):
        @pl.when(is_root)
        def _():
            take_copy(abuf, bbuf, take_sem, o, (c % spread) * cols, cols).wait()

    group = 2 * part
    for g in range(CHUNKS // 2):
        for q in (2 * g, 2 * g + 1):
            for o in range(owners):
                @pl.when(jnp.logical_not(is_root))
                def _():
                    b_copy(o, q, 0, False).wait_recv()

                right[...] = gated_product(
                    bbuf[o, q * part : (q + 1) * part].reshape(part * cols, -1),
                    gain_ref[...],
                    w_ref[:, 2 * hid : 4 * hid],
                )

                def swap(k, carry):
                    swapped[o * cols + k, q * part : (q + 1) * part] = right[
                        pl.ds(k, part, stride=cols), :
                    ]
                    return carry

                lax.fori_loop(0, cols, swap, 0, unroll=16)

        def multiply(t, carry):
            for j in range(0, group, 16):
                first = g * group + j

                def add(k8, sums):
                    sums = list(sums)
                    o = k8 // (cols // 8)
                    kk = (k8 % (cols // 8)) * 8
                    for k in range(8):
                        other = swapped[k8 * 8 + k, first : first + 16]
                        for i in range(8):
                            mine = left[t * 8 + i, o, pl.ds(kk + k, 1), :]
                            sums[i] = sums[i] + mine * other
                    return tuple(sums)

                sums = tuple(jnp.zeros((16, hid), jnp.float32) for _ in range(8))
                sums = lax.fori_loop(0, depth // 8, add, sums)
                for i in range(8):
                    product[t * 8 + i, j : j + 16] = sums[i]
            return carry

        lax.fori_loop(0, rows // 8, multiply, 0)
        some = min(rows, max(1, 512 // group))
        span = slice(g * group, (g + 1) * group)

        def finish(t, carry):
            at = pl.ds(t * some, some)
            flat = product[at].reshape(some * group, hid)
            middle = normalize(flat, mgain_ref[...]).astype(jnp.bfloat16)
            update = jnp.dot(middle, wout_ref[...], preferred_element_type=jnp.float32)
            update = update.reshape(some, group, -1) * gate[at, span]
            out_ref[at, span] = update.astype(jnp.bfloat16)
            return carry

        lax.fori_loop(0, rows // some, finish, 0)

    for o in range(owners):
        for q in range(CHUNKS):
            @pl.when(c == o)
            def _():
                each_a(o, q, lambda *at: a_copy(*at).wait_send())

            @pl.when(jnp.logical_and(chip != o // 2, c % 2 == q % 2))
            def _():
                sibling_copy(o, q).wait_send()

            each_b(o, q, lambda *at: b_copy(*at).wait_send())


def take_copy(abuf, bbuf, sem, o, first, count):
    return pltpu.make_async_copy(abuf.at[o, pl.ds(first, count)], bbuf.at[o], sem.at[o])


def body(mesh_sizes, pair_map, pair_mask, input_gain, input_weight, middle_gain, output_weight):
    n_row, n_col = mesh_sizes
    rows, cols, channels = pair_map.shape
    hid = output_weight.shape[0]
    owners = n_col // 4
    part = cols // CHUNKS
    vmem = pl.BlockSpec(memory_space=pltpu.VMEM)
    sizes = (rows, cols, owners, n_row, n_col, hid)
    f32, bf16 = jnp.float32, jnp.bfloat16
    dma = pltpu.SemaphoreType.DMA
    return pl.pallas_call(
        functools.partial(kernel, sizes),
        out_shape=jax.ShapeDtypeStruct(pair_map.shape, bf16),
        in_specs=[pl.BlockSpec(memory_space=pl.ANY)] + [vmem] * 5,
        out_specs=vmem,
        scratch_shapes=[
            pltpu.VMEM((rows, cols, channels), bf16),
            pltpu.VMEM((owners, rows, cols, channels), bf16),
            pltpu.VMEM((owners, cols, cols, channels), bf16),
            pltpu.VMEM((rows, owners, cols, hid), f32),
            pltpu.VMEM((part * cols, hid), f32),
            pltpu.VMEM((owners * cols, cols, hid), f32),
            pltpu.VMEM((rows, cols, channels), f32),
            pltpu.VMEM((rows, 2 * part, hid), f32),
            dma,
            dma((owners,)),
            dma((n_col, CHUNKS)),
            dma((owners, CHUNKS)),
            dma((owners, CHUNKS)),
            dma((owners, CHUNKS, 2, n_row)),
            dma((owners, CHUNKS)),
            dma((owners,)),
        ],
        compiler_params=pltpu.CompilerParams(
            collective_id=0, has_side_effects=True, vmem_limit_bytes=60 * 2**20
        ),
    )(
        pair_map,
        pair_mask,
        input_gain.reshape(1, -1),
        input_weight,
        middle_gain.reshape(1, -1),
        output_weight,
    )


def solution(mesh):
    placed = (P(("grp", "row"), "col", None), P(("grp", "row"), "col"), P(), P(), P(), P())
    return jax.shard_map(
        functools.partial(body, (mesh.shape["row"], mesh.shape["col"])),
        mesh=mesh,
        in_specs=placed,
        out_specs=P(("grp", "row"), "col", None),
        check_vma=False,
    )
```

time: 27.8 us -> 22.3 us (0.80)
  the two profiles are of different devices: /device:TPU:3 before, /device:TPU:2 now
where the time goes in v2:
time: 22.3 us; the launch traced here: 22.1 us
  Pallas kernels  20.5 us (92%)
  local copies, waits for them, and re-layouts  1.67 us (7%)
    pallas_call x1, Pallas kernels, body(): pl.pallas_call(functools.partial(kernel, sizes), out_shape=jax.ShapeDtype...  20.5 us
    unnamed x1, local copies, waits for them, and re-layouts  1.67 us

profile of v2, /device:TPU:2, one launch (start us, length us, event | category | flops | bytes accessed | tf_op | source)
XLA Modules:
  0.0 22.1 jit_solution(6192867180649965603)
XLA Ops:
  0.0 20.5 %shard_map.64 = bf16[32,32,128]{2,1,0:T(8,128)(2,1)} custom-call(bf16[32,32,128]{2,1,0:T(8,128)(2,1)} %x_hbm.1, s32[32,32]{1,0:T(8,128)} %mask_ref.1, f32[1,128]{1,0:T(1,128)} %bitcast.2, bf16[128,640]{1,0:T(8,128)(2,1)} %w_ref.1, f32[1,128]{1,0:T(1,128)} %bitcast.3, bf16[128,128]{1,0:T(8,128)(2,1)} %wout_ref.1), custom_call_target="tpu_custom_call" | custom-call | tf_op jit(solution)/shard_map/pallas_call | solution.py:304
  20.5 1.7 %copy.8 = bf16[32,32,128]{2,1,0:T(8,128)(2,1)} copy(bf16[32,32,128]{2,1,0:T(8,128)(2,1)} %shard_map.64) | data formatting | bytes 524288

commit v3 on v2

--- a/solution.py
+++ b/solution.py
@@ -10,6 +10,7 @@
 epsilon = 1e-05
 MESH = pl.DeviceIdType.MESH
 CHUNKS = 4
+ORDER = (3, 0, 1, 2)
 
 
 def normalize(values, gain_vector):
@@ -30,9 +31,10 @@
 
 
 def kernel(
-    sizes, x_hbm, mask_ref, gain_ref, w_ref, mgain_ref, wout_ref, out_ref,
+    sizes, x_hbm, mask_hbm, gain_hbm, w_hbm, mgain_hbm, wout_hbm, out_ref,
+    mask_ref, gain_ref, w_ref, mgain_ref, wout_ref,
     own, abuf, bbuf, left, right, swapped, gate, product,
-    own_sem, keep_sem, asend, arecv, fwd_send, bsend, brecv, take_sem,
+    own_sem, keep_sem, asend, arecv, fwd_send, bsend, brecv, take_sem, par_sem,
 ):
     rows, cols, owners, n_row, n_col, hid = sizes
     spread = n_col // n_row
@@ -51,8 +53,19 @@
     def crosses(one, other):
         return (one >= middle_row) != (other >= middle_row)
 
+    def first_across(of):
+        return jnp.where(of >= middle_row, middle_row - 1, middle_row)
+
+    def helped(of, q):
+        if q == CHUNKS - 1:
+            return of >= 0
+        return (of >= middle_row) if q % 2 else (of < 0)
+
+    across = crosses(r, root)
+    entry = first_across(root)
+    relays = jnp.logical_and(across, r == entry)
+
     own_copy = pltpu.make_async_copy(x_hbm, own, own_sem)
-    own_copy.start()
 
     barrier = pltpu.get_barrier_semaphore()
     owner_chips = (owners + 1) // 2
@@ -63,9 +76,9 @@
 
     @pl.when(jnp.logical_not(is_root))
     def _():
-        greet({"row": root})
-
-    @pl.when(crosses(r, root))
+        greet({"row": jnp.where(jnp.logical_and(across, r != entry), entry, root)})
+
+    @pl.when(across)
     def _():
         greet({"row": root, "col": partner})
 
@@ -78,11 +91,27 @@
     def _():
         greet({"col": sibling})
 
+    own_copy.start()
+    params = [
+        pltpu.make_async_copy(a, b, par_sem.at[i])
+        for i, (a, b) in enumerate(
+            [
+                (mask_hbm, mask_ref),
+                (gain_hbm, gain_ref),
+                (w_hbm, w_ref),
+                (mgain_hbm, mgain_ref),
+                (wout_hbm, wout_ref),
+            ]
+        )
+    ]
+    for copy in params:
+        copy.start()
     helps = r == partner_root
     awaited = (
         jnp.where(c < owners, n_col - 1, 0)
         + forwards.astype(jnp.int32)
-        + jnp.where(is_root, n_row - 1, 0)
+        + jnp.where(is_root, middle_row, 0)
+        + jnp.where(relays, middle_row - 1, 0)
         + jnp.where(helps, middle_row, 0)
     )
 
@@ -124,17 +153,39 @@
 
     def each_b(o, q, act):
         for row in range(n_row):
+            to_entry = jnp.logical_and(row == entry, jnp.logical_not(helped(root, q)))
+            near = jnp.logical_not(crosses(root, row))
             direct = jnp.logical_and(is_root, root != row)
-            if q % 2:
-                direct = jnp.logical_and(direct, jnp.logical_not(crosses(root, row)))
-
-                @pl.when(jnp.logical_and(helps, crosses(partner_root, row)))
-                def _():
-                    act(o, q, row, True)
+            direct = jnp.logical_and(direct, jnp.logical_or(near, to_entry))
+            help_it = jnp.logical_and(helps, crosses(partner_root, row))
+
+            @pl.when(jnp.logical_and(help_it, helped(partner_root, q)))
+            def _():
+                act(o, q, row, True)
 
             @pl.when(direct)
             def _():
                 act(o, q, row, False)
+
+    def relay_copy(o, q, row):
+        at = pl.ds(q * part, part)
+        return pltpu.make_async_remote_copy(
+            src_ref=bbuf.at[o, at],
+            dst_ref=bbuf.at[o, at],
+            send_sem=bsend.at[o, q, 0, row],
+            recv_sem=brecv.at[o, q],
+            device_id={"row": row},
+            device_id_type=MESH,
+        )
+
+    def each_relay(o, q, act):
+        for row in range(n_row):
+            onward = jnp.logical_and(crosses(root, row), row != entry)
+            onward = jnp.logical_and(onward, jnp.logical_not(helped(root, q)))
+
+            @pl.when(jnp.logical_and(relays, onward))
+            def _():
+                act(o, q, row)
 
     def start_b(o, q):
         @pl.when(c == o)
@@ -157,11 +208,11 @@
         @pl.when(c == o)
         def _():
             keep[o].start()
-            for q in range(CHUNKS):
+            for q in ORDER:
                 each_a(o, q, lambda *at: a_copy(*at).start())
 
     for o in range(owners):
-        for q in range(CHUNKS):
+        for q in ORDER:
             @pl.when(c != o)
             def _():
                 a_copy(o, q, 0).wait_recv()
@@ -185,6 +236,8 @@
             take_copy(abuf, bbuf, take_sem, o, (c % spread) * cols, cols).start()
 
     own_copy.wait()
+    for copy in params:
+        copy.wait()
     step = min(rows, max(1, 512 // cols))
 
     def gate_step(t, carry):
@@ -212,6 +265,12 @@
         lax.fori_loop(0, rows // step, left_step, 0)
 
     for o in range(owners):
+        @pl.when(relays)
+        def _():
+            for q in range(CHUNKS):
+                b_copy(o, q, 0, False).wait_recv()
+                each_relay(o, q, lambda *at: relay_copy(*at).start())
+
         @pl.when(is_root)
         def _():
             take_copy(abuf, bbuf, take_sem, o, (c % spread) * cols, cols).wait()
@@ -220,7 +279,7 @@
     for g in range(CHUNKS // 2):
         for q in (2 * g, 2 * g + 1):
             for o in range(owners):
-                @pl.when(jnp.logical_not(is_root))
+                @pl.when(jnp.logical_not(jnp.logical_or(is_root, relays)))
                 def _():
                     b_copy(o, q, 0, False).wait_recv()
 
@@ -285,6 +344,7 @@
                 sibling_copy(o, q).wait_send()
 
             each_b(o, q, lambda *at: b_copy(*at).wait_send())
+            each_relay(o, q, lambda *at: relay_copy(*at).wait_send())
 
 
 def take_copy(abuf, bbuf, sem, o, first, count):
@@ -304,9 +364,14 @@
     return pl.pallas_call(
         functools.partial(kernel, sizes),
         out_shape=jax.ShapeDtypeStruct(pair_map.shape, bf16),
-        in_specs=[pl.BlockSpec(memory_space=pl.ANY)] + [vmem] * 5,
+        in_specs=[pl.BlockSpec(memory_space=pl.ANY)] * 6,
         out_specs=vmem,
         scratch_shapes=[
+            pltpu.VMEM(pair_mask.shape, pair_mask.dtype),
+            pltpu.VMEM((1, channels), f32),
+            pltpu.VMEM(input_weight.shape, bf16),
+            pltpu.VMEM((1, hid), f32),
+            pltpu.VMEM(output_weight.shape, bf16),
             pltpu.VMEM((rows, cols, channels), bf16),
             pltpu.VMEM((owners, rows, cols, channels), bf16),
             pltpu.VMEM((owners, cols, cols, channels), bf16),
@@ -323,6 +388,7 @@
             dma((owners, CHUNKS, 2, n_row)),
             dma((owners, CHUNKS)),
             dma((owners,)),
+            dma((5,)),
         ],
         compiler_params=pltpu.CompilerParams(
             collective_id=0, has_side_effects=True, vmem_limit_bytes=60 * 2**20

time: 22.3 us -> 21.6 us (0.969)
  the two profiles are of different devices: /device:TPU:2 before, /device:TPU:3 now
where the time goes in v3:
time: 21.6 us; the launch traced here: 21.4 us
  Pallas kernels  19.8 us (92%)
  local copies, waits for them, and re-layouts  1.67 us (8%)
    pallas_call x1, Pallas kernels, body(): pl.pallas_call(functools.partial(kernel, sizes), out_shape=jax.ShapeDtype...  19.8 us
    unnamed x1, local copies, waits for them, and re-layouts  1.67 us

profile of v3, /device:TPU:3, one launch (start us, length us, event | category | flops | bytes accessed | tf_op | source)
XLA Modules:
  0.0 21.4 jit_solution(5935986656073832421)
XLA Ops:
  0.0 19.8 %shard_map.64 = bf16[32,32,128]{2,1,0:T(8,128)(2,1)} custom-call(bf16[32,32,128]{2,1,0:T(8,128)(2,1)} %x_hbm.1, s32[32,32]{1,0:T(8,128)} %mask_hbm.1, f32[1,128]{1,0:T(1,128)} %bitcast.2, bf16[128,640]{1,0:T(8,128)(2,1)} %w_hbm.1, f32[1,128]{1,0:T(1,128)} %bitcast.3, bf16[128,128]{1,0:T(8,128)(2,1)} %wout_hbm.1), custom_call_target="tpu_custom_call" | custom-call | tf_op jit(solution)/shard_map/pallas_call | solution.py:364
  19.8 1.7 %copy.8 = bf16[32,32,128]{2,1,0:T(8,128)(2,1)} copy(bf16[32,32,128]{2,1,0:T(8,128)(2,1)} %shard_map.64) | data formatting | bytes 524288

commit v4 on v3

--- a/solution.py
+++ b/solution.py
@@ -10,7 +10,7 @@
 epsilon = 1e-05
 MESH = pl.DeviceIdType.MESH
 CHUNKS = 4
-ORDER = (3, 0, 1, 2)
+ORDER = (0, 2, 3, 1)
 
 
 def normalize(values, gain_vector):
@@ -63,7 +63,8 @@
 
     across = crosses(r, root)
     entry = first_across(root)
-    relays = jnp.logical_and(across, r == entry)
+    relayed = root < middle_row
+    relays = jnp.logical_and(jnp.logical_and(across, relayed), r == entry)
 
     own_copy = pltpu.make_async_copy(x_hbm, own, own_sem)
 
@@ -76,7 +77,7 @@
 
     @pl.when(jnp.logical_not(is_root))
     def _():
-        greet({"row": jnp.where(jnp.logical_and(across, r != entry), entry, root)})
+        greet({"row": jnp.where(jnp.logical_and(jnp.logical_and(across, relayed), r != entry), entry, root)})
 
     @pl.when(across)
     def _():
@@ -110,7 +111,7 @@
     awaited = (
         jnp.where(c < owners, n_col - 1, 0)
         + forwards.astype(jnp.int32)
-        + jnp.where(is_root, middle_row, 0)
+        + jnp.where(is_root, jnp.where(relayed, middle_row, n_row - 1), 0)
         + jnp.where(relays, middle_row - 1, 0)
         + jnp.where(helps, middle_row, 0)
     )
@@ -153,7 +154,8 @@
 
     def each_b(o, q, act):
         for row in range(n_row):
-            to_entry = jnp.logical_and(row == entry, jnp.logical_not(helped(root, q)))
+            to_entry = jnp.logical_or(row == entry, jnp.logical_not(relayed))
+            to_entry = jnp.logical_and(to_entry, jnp.logical_not(helped(root, q)))
             near = jnp.logical_not(crosses(root, row))
             direct = jnp.logical_and(is_root, root != row)
             direct = jnp.logical_and(direct, jnp.logical_or(near, to_entry))
@@ -188,11 +190,11 @@
                 act(o, q, row)
 
     def start_b(o, q):
-        @pl.when(c == o)
+        @pl.when(jnp.logical_and(jnp.logical_or(is_root, helps), c == o))
         def _():
             each_b(o, q, lambda *at: b_copy(*at, from_own=True).start())
 
-        @pl.when(c != o)
+        @pl.when(jnp.logical_and(jnp.logical_or(is_root, helps), c != o))
         def _():
             each_b(o, q, lambda *at: b_copy(*at).start())
 
@@ -200,9 +202,15 @@
 
     def each_a(o, q, act):
         for target in range(n_col):
-            if target == o or (target // 2 != o // 2 and target % 2 != q % 2):
+            if target == o:
                 continue
-            act(o, q, target)
+            if target // 2 == o // 2:
+                act(o, q, target)
+                continue
+
+            @pl.when((q + r) % 2 == target % 2)
+            def _():
+                act(o, q, target)
 
     for o in range(owners):
         @pl.when(c == o)
@@ -210,30 +218,6 @@
             keep[o].start()
             for q in ORDER:
                 each_a(o, q, lambda *at: a_copy(*at).start())
-
-    for o in range(owners):
-        for q in ORDER:
-            @pl.when(c != o)
-            def _():
-                a_copy(o, q, 0).wait_recv()
-
-            @pl.when(jnp.logical_and(chip != o // 2, c % 2 == q % 2))
-            def _():
-                sibling_copy(o, q).start()
-
-            if spread == 1:
-                start_b(o, q)
-        if spread != 1:
-            for q in range(CHUNKS):
-                start_b(o, q)
-
-        @pl.when(c == o)
-        def _():
-            keep[o].wait()
-
-        @pl.when(is_root)
-        def _():
-            take_copy(abuf, bbuf, take_sem, o, (c % spread) * cols, cols).start()
 
     own_copy.wait()
     for copy in params:
@@ -252,6 +236,30 @@
         return carry
 
     lax.fori_loop(0, rows // step, gate_step, 0)
+
+    for o in range(owners):
+        for q in ORDER:
+            @pl.when(c != o)
+            def _():
+                a_copy(o, q, 0).wait_recv()
+
+            @pl.when(jnp.logical_and(chip != o // 2, c % 2 == (q + r) % 2))
+            def _():
+                sibling_copy(o, q).start()
+
+            if spread == 1:
+                start_b(o, q)
+        if spread != 1:
+            for q in range(CHUNKS):
+                start_b(o, q)
+
+        @pl.when(c == o)
+        def _():
+            keep[o].wait()
+
+        @pl.when(is_root)
+        def _():
+            take_copy(abuf, bbuf, take_sem, o, (c % spread) * cols, cols).start()
 
     for o in range(owners):
         def left_step(t, carry):
@@ -334,17 +342,25 @@
         lax.fori_loop(0, rows // some, finish, 0)
 
     for o in range(owners):
+        @pl.when(c == o)
+        def _():
+            for q in range(CHUNKS):
+                each_a(o, q, lambda *at: a_copy(*at).wait_send())
+
         for q in range(CHUNKS):
-            @pl.when(c == o)
-            def _():
-                each_a(o, q, lambda *at: a_copy(*at).wait_send())
-
-            @pl.when(jnp.logical_and(chip != o // 2, c % 2 == q % 2))
+            @pl.when(jnp.logical_and(chip != o // 2, c % 2 == (q + r) % 2))
             def _():
                 sibling_copy(o, q).wait_send()
 
-            each_b(o, q, lambda *at: b_copy(*at).wait_send())
-            each_relay(o, q, lambda *at: relay_copy(*at).wait_send())
+        @pl.when(jnp.logical_or(is_root, helps))
+        def _():
+            for q in range(CHUNKS):
+                each_b(o, q, lambda *at: b_copy(*at).wait_send())
+
+        @pl.when(relays)
+        def _():
+            for q in range(CHUNKS):
+                each_relay(o, q, lambda *at: relay_copy(*at).wait_send())
 
 
 def take_copy(abuf, bbuf, sem, o, first, count):

time: 21.6 us -> 20 us (0.926)
  the two profiles are of different devices: /device:TPU:3 before, /device:TPU:24 now
where the time goes in v4:
time: 20 us; the launch traced here: 19.9 us
  Pallas kernels  18.2 us (91%)
  local copies, waits for them, and re-layouts  1.67 us (8%)
    pallas_call x1, Pallas kernels, body(): pl.pallas_call(functools.partial(kernel, sizes), out_shape=jax.ShapeDtype...  18.2 us
    unnamed x1, local copies, waits for them, and re-layouts  1.67 us

profile of v4, /device:TPU:24, one launch (start us, length us, event | category | flops | bytes accessed | tf_op | source)
XLA Modules:
  0.0 19.9 jit_solution(16783013778974770164)
XLA Ops:
  0.0 18.2 %shard_map.64 = bf16[32,32,128]{2,1,0:T(8,128)(2,1)} custom-call(bf16[32,32,128]{2,1,0:T(8,128)(2,1)} %x_hbm.1, s32[32,32]{1,0:T(8,128)} %mask_hbm.1, f32[1,128]{1,0:T(1,128)} %bitcast.2, bf16[128,640]{1,0:T(8,128)(2,1)} %w_hbm.1, f32[1,128]{1,0:T(1,128)} %bitcast.3, bf16[128,128]{1,0:T(8,128)(2,1)} %wout_hbm.1), custom_call_target="tpu_custom_call" | custom-call | tf_op jit(solution)/shard_map/pallas_call | solution.py:380
  18.2 1.7 %copy.8 = bf16[32,32,128]{2,1,0:T(8,128)(2,1)} copy(bf16[32,32,128]{2,1,0:T(8,128)(2,1)} %shard_map.64) | data formatting | bytes 524288
